TPU v7x, 32 devices: a whole 2x2x4 slice. The times are simulated.
32 devices in a mesh: groups: 2 (over x), wide: 16 (over z, y, core).
Axes of the slice: x: 2, y: 2, z: 4, core: 2. Of those that a mesh axis runs over, the one named last changes fastest.
Arguments:
- loader_features: bfloat16 [32768, 128], P(('groups', 'wide')), parts along dimension 0, may hold values from -6 to 6
- dest: int32 [32768], P(('groups', 'wide')), parts along dimension 0, may hold values from 0 to 16383, as said below
- block_values: bfloat16 [8192, 128, 128], P(('groups', 'wide')), parts along dimension 0, may hold values from -0.09375 to 0.09375
- row_block: int32 [8192], P(('groups', 'wide')), parts along dimension 0, may hold values from 0 to 7, as said below
- col_block: int32 [8192], P(('groups', 'wide')), parts along dimension 0, may hold values from 0 to 127, as said below
- w_first: bfloat16 [128, 256], replicated, may hold values from -0.5 to 0.5
- b_first: float32 [256], replicated, may hold values from -3 to 3
- w_second: bfloat16 [256, 256], replicated, may hold values from -0.375 to 0.375
- b_second: float32 [256], replicated, may hold values from -3 to 3
Outputs:
- output: bfloat16 [32768, 256], P(('groups', 'wide')), parts along dimension 0
There are 2 independent parts, one for each index of `groups`. A program takes and returns all parts, laid end to end along the dimension named above; an argument that names none is the same for every part. Nothing has to cross between parts.
Inputs may be any that keep to these rules, and one draw needn't show every extreme that they name: dest is a permutation; row i goes to owner dest[i] // 1024. Each device sends at most 256 of its rows to one owner and exactly 256 to some owner; every owner receives exactly 256 rows from some device. `col_block`: A device's list holds 16 groups of 16 entries; in group g every column block lies in device g's nodes (g * 8 to g * 8 + 7); the k-th entry's column block depends only on k mod 2, and these 2 are distinct. `row_block`: in each group, the k-th entry's row block is distinct among entries with the same k mod 2.
All inputs are finite; a program needn't handle non-finite values.
Results may differ from a plain program's by a relative error of at most 0.0058.
Values may be sent and summed in bfloat16 or wider, within the bound.
A program may use at most 128 MiB of HBM per device.

v0:
```python
import math
import jax
import jax.numpy as jnp
from jax import lax
from jax.sharding import PartitionSpec as P


def body(
    loader_features, dest, block_values, row_block, col_block, w_first, b_first, w_second, b_second
):
    devices = lax.axis_size("wide")
    own_index = lax.axis_index("wide")
    node_dev = loader_features.shape[0]
    feature_width = loader_features.shape[1]
    block_size = block_values.shape[1]
    row_blocks = node_dev // block_size
    slots = block_values.shape[0] // devices
    used = slots // row_blocks
    batch_groups = math.gcd(devices, 8)
    all_rows = lax.all_gather(loader_features, "wide", axis=0, tiled=True)
    all_dest = lax.all_gather(dest, "wide", axis=0, tiled=True)
    local = all_dest - own_index * node_dev
    local = jnp.where((local >= 0) & (local < node_dev), local, node_dev)
    features = (
        jnp.zeros((node_dev + 1, feature_width), jnp.bfloat16).at[local].set(all_rows)[:node_dev]
    )
    grid_rows = row_block.reshape(devices, row_blocks, used)
    order = jnp.argsort(grid_rows, axis=1, stable=True)
    grid_values = block_values.reshape(devices, row_blocks, used, block_size, block_size)
    ordered = jnp.take_along_axis(grid_values, order[:, :, :, None, None], axis=1)
    group_cols = col_block.reshape(devices, row_blocks, used)[:, 0, :]

    def aggregate(panel):
        width = panel.shape[1]
        empty = jnp.zeros((row_blocks, block_size, width), jnp.float32)
        carry = empty
        piece = lax.all_gather(panel, "wide", axis=0, tiled=True)
        start = jnp.int32(0)
        length = piece.shape[0]
        tile_count = length // block_size
        piece_tiles = piece.reshape(tile_count, block_size, width)
        first_group = start // node_dev
        covered = -(-length // node_dev) + 0
        covered = min(devices, covered)
        span = min(covered, batch_groups)
        for batch in range(-(-covered // span)):
            wanted_group = first_group + batch * span
            begin = jnp.minimum(wanted_group, devices - span)
            values = lax.dynamic_slice_in_dim(ordered, begin, span, 0)
            cols = lax.dynamic_slice_in_dim(group_cols, begin, span, 0)
            group_of = begin + jnp.arange(span, dtype=jnp.int32)
            valid = (cols >= 0) & (cols < tile_count) & (group_of[:, None] >= wanted_group)
            picked = jnp.take(piece_tiles, jnp.clip(cols, 0, tile_count - 1), axis=0)
            picked = picked * valid.astype(jnp.bfloat16)[:, :, None, None]
            carry = carry + jnp.einsum(
                "gruij,gujw->riw", values, picked, preferred_element_type=jnp.float32
            )
        return carry.reshape(node_dev, width)

    first = aggregate(features).astype(jnp.bfloat16)
    hidden = jax.nn.relu(
        jnp.dot(first, w_first, preferred_element_type=jnp.float32) + b_first
    ).astype(jnp.bfloat16)
    second = aggregate(hidden).astype(jnp.bfloat16)
    output = jnp.dot(second, w_second, preferred_element_type=jnp.float32) + b_second
    return output.astype(jnp.bfloat16)


def solution(mesh):
    placed = (
        P(("groups", "wide"), None),
        P(("groups", "wide")),
        P(("groups", "wide"), None, None),
        P(("groups", "wide")),
        P(("groups", "wide")),
        P(),
        P(),
        P(),
        P(),
    )
    return jax.shard_map(
        body, mesh=mesh, in_specs=placed, out_specs=P(("groups", "wide"), None), check_vma=False
    )
```

profile of v0, /device:TPU:0, one launch (start us, length us, event | category | flops | bytes accessed | tf_op | source)
XLA Modules:
  0.0 262.6 jit_solution(10796248333810704136)
XLA Ops:
  6.5 0.7 all-gather.4.cloned.1.call-update
  7.3 23.6 %all_gather.12 = s32[16384]{0:T(1024)S(1)} all-gather(s32[1024]{0:T(1024)} %param.14), channel_id=1, replica_groups=mesh['groups'=2,'wide'=16] {'wide'}, dimensions={0}, use_global_device_ids=true | all-gather | bytes 69632 | tf_op jit(solution)/shard_map/all_gather | solution.py:21
  31.0 31.9 %all-gather.4.cloned.1.call-done = bf16[16384,128]{1,0:T(8,128)(2,1)} async-done(((bf16[1024,128]{1,0:T(8,128)(2,1)}), bf16[16384,128]{1,0:T(8,128)(2,1)}) %all-gather.4.cloned.1.call-update) | async-done | bytes 4194320 | tf_op jit(solution)/shard_map/all_gather | solution.py:20
  62.9 41.4 %scatter_custom_fusion = bf16[1025,128]{1,0:T(8,128)(2,1)S(1)} fusion(s32[16384]{0:T(1024)S(1)} %compare_select_fusion, bf16[16384,128]{1,0:T(8,128)(2,1)} %all-gather.4.cloned.1.call-done, bf16[]{:T(256)} %constant.78.clone.1), kind=kCustom, calls=%fused_computation.50 | custom fusion | bytes 262912 | tf_op jit(solution)/shard_map/scatter | solution.py:25
  104.3 0.7 slice.22
  105.1 0.8 reshape.122
  105.9 0.8 reshape.126
  106.8 0.1 copy.79
  106.9 0.1 copy.57
  107.1 0.1 copy.62
  107.2 0.1 copy.60
  107.3 0.1 copy.64
  107.4 0.1 copy.59
  107.4 0.1 reshape.189
  107.5 0.1 copy.63
  107.7 5.3 %sort.17 = (s32[16,8,2]{2,1,0:T(8,128)}, s32[16,8,2]{2,1,0:T(8,128)S(1)}) sort(s32[16,8,2]{2,1,0:T(8,128)S(1)} %reshape.122, s32[16,8,2]{2,1,0:T(8,128)S(1)} %iota.16), dimensions={1}, to_apply=%region_0.1 | sort | flops 2048 | bytes 4096 | tf_op jit(solution)/shard_map/jit(argsort)/sort | solution.py:28
  113.0 0.1 reshape.161
  113.1 14.2 %gather_fusion = bf16[256,128,128]{2,1,0:T(8,128)(2,1)} fusion(bf16[16,8,2,128,128]{4,3,2,1,0:T(8,128)(2,1)} %bitcast.79, s32[256]{0:T(256)S(1)} %reshape.161), kind=kCustom, calls=%fused_computation.4 | custom fusion | bytes 16780288 | tf_op jit(solution)/shard_map/jit(take_along_axis)/gather | solution.py:30
  127.4 27.0 %all-gather.6.cloned.1.call-done = bf16[16384,128]{1,0:T(8,128)(2,1)} async-done(((bf16[1024,128]{1,0:T(8,128)(2,1)}), bf16[16384,128]{1,0:T(8,128)(2,1)}) %all-gather.6.cloned.1.call-update) | async-done | bytes 4194320 | tf_op jit(solution)/shard_map/all_gather | solution.py:37
  154.4 2.8 %gather_fusion.1 = bf16[16,128,128]{2,1,0:T(8,128)(2,1)S(1)} fusion(bf16[128,128,128]{2,1,0:T(8,128)(2,1)} %bitcast.93, s32[1024]{0:T(1024)S(1)} %pad_clamp_fusion.1), kind=kCustom, calls=%fused_computation.clone | custom fusion | bytes 1048640 | tf_op jit(solution)/shard_map/jit(_take)/gather | solution.py:53
  157.3 2.8 %gather_fusion.2 = bf16[16,128,128]{2,1,0:T(8,128)(2,1)S(1)} fusion(bf16[128,128,128]{2,1,0:T(8,128)(2,1)} %bitcast.94, s32[1024]{0:T(1024)S(1)} %pad_clamp_fusion), kind=kCustom, calls=%fused_computation.2.clone | custom fusion | bytes 1048640 | tf_op jit(solution)/shard_map/jit(_take)/gather | solution.py:53
  160.1 3.7 %fusion.15 = f32[8,128,128]{2,1,0:T(8,128)S(1)} fusion(bf16[16,8,2,128,128]{4,3,2,1,0:T(8,128)(2,1)} %bitcast.80, pred[16,8,2]{2,1,0:T(8,128)(4,1)S(1)} %compare_and_fusion, bf16[8,2,128,128]{3,2,1,0:T(8,128)(2,1)S(1)} %bitcast.91, pred[8,2]{1,0:T(8,128)(4,1)S(1)} %copy.57, bf16[8,2]{1,0:T(8,128)(2,1)S(1)} %copy.60), kind=kOutput, calls=%fused_computation.24 | convolution fusion | flops 542375936 | bytes 9437488 | tf_op jit(solution)/shard_map/gruij,gujw->riw/dot_general | solution.py:55
  163.8 0.9 copy-done.1
  164.8 1.4 fusion.18
  166.2 1.1 fusion.13
  167.3 73.5 %all-gather.8.cloned.1.call-done = bf16[16384,256]{1,0:T(8,128)(2,1)} async-done(((bf16[1024,256]{1,0:T(8,128)(2,1)}), bf16[16384,256]{1,0:T(8,128)(2,1)}) %all-gather.8.cloned.1.call-update) | async-done | bytes 8388624 | tf_op jit(solution)/shard_map/all_gather | solution.py:37
  240.8 4.0 %gather_fusion.4 = bf16[16,128,256]{2,1,0:T(8,128)(2,1)S(1)} fusion(bf16[128,128,256]{2,1,0:T(8,128)(2,1)} %bitcast.88, s32[1024]{0:T(1024)S(1)} %pad_clamp_fusion), kind=kCustom, calls=%fused_computation.3.clone | custom fusion | bytes 2097216 | tf_op jit(solution)/shard_map/jit(_take)/gather | solution.py:53
  244.8 4.0 %gather_fusion.3 = bf16[16,128,256]{2,1,0:T(8,128)(2,1)S(1)} fusion(bf16[128,128,256]{2,1,0:T(8,128)(2,1)} %bitcast.89, s32[1024]{0:T(1024)S(1)} %pad_clamp_fusion.1), kind=kCustom, calls=%fused_computation.1.clone | custom fusion | bytes 2097216 | tf_op jit(solution)/shard_map/jit(_take)/gather | solution.py:53
  248.8 3.7 %fusion.8 = f32[8,128,256]{2,1,0:T(8,128)S(1)} fusion(bf16[16,8,2,128,128]{4,3,2,1,0:T(8,128)(2,1)} %bitcast.81, pred[16,8,2]{2,1,0:T(8,128)(4,1)S(1)} %compare_and_fusion, bf16[8,2,128,256]{3,2,1,0:T(8,128)(2,1)S(1)} %bitcast.87, pred[8,2]{1,0:T(8,128)(4,1)S(1)} %copy.57, bf16[8,2]{1,0:T(8,128)(2,1)S(1)} %copy.60), kind=kOutput, calls=%fused_computation.15 | convolution fusion | flops 1080557568 | bytes 10486064 | tf_op jit(solution)/shard_map/gruij,gujw->riw/dot_general | solution.py:55
  252.6 1.0 slice-done.1
  253.5 1.4 fusion.12
  255.0 1.1 fusion.14
  (33 shorter events, 0.4 us)
Async XLA Ops:
  6.5 248.4 %copy-start = (bf16[256,256]{1,0:T(8,128)(2,1)S(1)}, bf16[256,256]{1,0:T(8,128)(2,1)}, u32[]{:S(2)}) copy-start(bf16[256,256]{1,0:T(8,128)(2,1)} %param.20) | copy-start | bytes 393220
  6.5 56.4 %all-gather.4.cloned.1.call-start = ((), (), s32[]{:S(2)}) async-start(), calls=%async_computation | async-start | bytes 4456448 | tf_op jit(solution)/shard_map/all_gather | solution.py:20
  7.3 147.2 %all-gather.6.cloned.1.call-start = ((), (), s32[]{:S(2)}) async-start(), calls=%async_computation.1 | async-start | bytes 4456448 | tf_op jit(solution)/shard_map/all_gather | solution.py:37
  105.1 135.8 %all-gather.8.cloned.1.call-start = ((), (), s32[]{:S(2)}) async-start(), calls=%async_computation.2 | async-start | bytes 8912896 | tf_op jit(solution)/shard_map/all_gather | solution.py:37
  160.1 4.6 %copy-start.1 = (bf16[256,128,128]{2,1,0:T(8,128)(2,1)S(1)}, bf16[256,128,128]{2,1,0:T(8,128)(2,1)}, u32[]{:S(2)}) copy-start(bf16[256,128,128]{2,1,0:T(8,128)(2,1)} %gather_fusion) | copy-start | bytes 25165828
  160.1 6.0 %copy-start.2 = (bf16[128,256]{1,0:T(8,128)(2,1)S(1)}, bf16[128,256]{1,0:T(8,128)(2,1)}, u32[]{:S(2)}) copy-start(bf16[128,256]{1,0:T(8,128)(2,1)} %param.18) | copy-start | bytes 196612
  160.1 6.0 %copy-start.3 = (f32[256]{0:T(256)S(1)}, f32[256]{0:T(256)}, u32[]{:S(2)}) copy-start(f32[256]{0:T(256)} %param.19) | copy-start | bytes 3076
  248.8 3.8 %slice-start = ((s8[8388608]{0:T(1024)(128)(4,1)}), s8[4194304]{0:T(1024)(128)(4,1)S(1)}, s32[]{:S(2)}) async-start(s8[8388608]{0:T(1024)(128)(4,1)} %bitcast.83), calls=%async_computation.3 | async-start | bytes 8388608
  248.8 4.7 %slice-start.1 = ((s8[8388608]{0:T(1024)(128)(4,1)}), s8[4194304]{0:T(1024)(128)(4,1)S(1)}, s32[]{:S(2)}) async-start(s8[8388608]{0:T(1024)(128)(4,1)} %bitcast.83), calls=%async_computation.4 | async-start | bytes 8388608
  253.5 1.4 copy-start.4
Sparse Core Ops, SparseCore 0:
  9.5 53.3 all-gather.3
  105.2 49.2 all-gather.5
  167.4 73.3 all-gather.7
where the time goes:
time: 263 us
  waiting for transfers between devices  133 us (51%)
  local copies, waits for them, and re-layouts  74.5 us (28%)
  blocking collectives  23.6 us (9%)
  between operations  13.3 us (5%)
  matrix products  12.4 us (5%)
  other arithmetic  5.39 us (2%)
    all_gather x2, waiting for transfers between devices, aggregate(): piece = lax.all_gather(panel, 'wide', axis=0, tiled=True)  101 us
    scatter x1, local copies, waits for them, and re-layouts, body(): jnp.zeros((node_dev + 1, feature_width), jnp.bfloat16).at[local]  41.4 us
    all_gather x1, waiting for transfers between devices, body(): all_rows = lax.all_gather(loader_features, 'wide', axis=0, tiled=True)  31.9 us
    all_gather x1, blocking collectives, body(): all_dest = lax.all_gather(dest, 'wide', axis=0, tiled=True)  23.6 us
    gather x2, local copies, waits for them, and re-layouts, body(): jnp.take_along_axis(grid_values, order[:, :, :, None, None], axis=1)  14.3 us
    gather x4, local copies, waits for them, and re-layouts, aggregate(): picked = jnp.take(piece_tiles, jnp.clip(cols, 0, tile_count - 1), axis=0)  13.7 us
    dot_general x4, matrix products, aggregate(): jnp.einsum('gruij,gujw->riw', values, picked, preferred_element_type=jnp....  10.2 us
    sort x1, other arithmetic, body(): order = jnp.argsort(grid_rows, axis=1, stable=True)  5.26 us
  transfers between devices with their start and end apart: 3, of which 3 were waited for; matrix products, arithmetic and copies ran while one was open for 8% of the time, Pallas kernels for 0%

commit v1 on v0

--- a/solution.py
+++ b/solution.py
@@ -3,6 +3,18 @@
 import jax.numpy as jnp
 from jax import lax
 from jax.sharding import PartitionSpec as P
+
+
+def gather_by_bits(x, axis, dim):
+    ways, here = (lax.axis_size(axis), lax.axis_index(axis))
+    grown, reach = (x, 1)
+    while reach < ways:
+        theirs = lax.ppermute(grown, axis, [(d, d ^ reach) for d in range(ways)])
+        mine_first = jnp.concatenate([grown, theirs], axis=dim)
+        theirs_first = jnp.concatenate([theirs, grown], axis=dim)
+        grown = jnp.where(here & reach == 0, mine_first, theirs_first)
+        reach = 2 * reach
+    return grown
 
 
 def body(
@@ -17,7 +29,7 @@
     slots = block_values.shape[0] // devices
     used = slots // row_blocks
     batch_groups = math.gcd(devices, 8)
-    all_rows = lax.all_gather(loader_features, "wide", axis=0, tiled=True)
+    all_rows = gather_by_bits(loader_features, "wide", 0)
     all_dest = lax.all_gather(dest, "wide", axis=0, tiled=True)
     local = all_dest - own_index * node_dev
     local = jnp.where((local >= 0) & (local < node_dev), local, node_dev)

time: 263 us -> 371 us (1.41)
  other arithmetic: 5.39 us -> 64.8 us
  waiting for transfers between devices: 133 us -> 180 us
  local copies, waits for them, and re-layouts: 74.5 us -> 30.8 us
  blocking collectives: 23.6 us -> 59.4 us
  starting transfers between devices: 0.08 us -> 8.05 us
    ppermute x0 -> x4, waiting for transfers between devices: none -> 67 us  [gather_by_bits(): theirs = lax.ppermute(grown, axis, [(d, d ^ reach) for d in range(ways)])]
    scatter x0 -> x1, other arithmetic: none -> 55.9 us  [body(): jnp.zeros((node_dev + 1, feature_width), jnp.bfloat16).at[local]]
    scatter x1 -> x0, local copies, waits for them, and re-layouts: 41.4 us -> none  [body(): jnp.zeros((node_dev + 1, feature_width), jnp.bfloat16).at[local]]
    all_gather x1, blocking collectives: 23.6 us -> 59.4 us  [body(): all_dest = lax.all_gather(dest, 'wide', axis=0, tiled=True)]
    all_gather x1 -> x0, waiting for transfers between devices: 31.9 us -> none  [body(): all_rows = lax.all_gather(loader_features, 'wide', axis=0, tiled=True)]
    all_gather x2, waiting for transfers between devices: 101 us -> 113 us  [aggregate(): piece = lax.all_gather(panel, 'wide', axis=0, tiled=True)]
    ppermute x0 -> x4, starting transfers between devices: none -> 7.82 us  [gather_by_bits(): theirs = lax.ppermute(grown, axis, [(d, d ^ reach) for d in range(ways)])]
  transfers between devices with their start and end apart: 3 -> 6, of which waited for: 3 -> 6; matrix products, arithmetic and copies ran while one was open for 8% -> 6% of each run, Pallas kernels for 0% -> 0%
where the time goes in v1:
time: 371 us
  waiting for transfers between devices  180 us (49%)
  other arithmetic  64.8 us (17%)
  blocking collectives  59.4 us (16%)
  local copies, waits for them, and re-layouts  30.8 us (8%)
  matrix products  14.4 us (4%)
  between operations  13.6 us (4%)
  starting transfers between devices  8.05 us (2%)
    all_gather x2, waiting for transfers between devices, aggregate(): piece = lax.all_gather(panel, 'wide', axis=0, tiled=True)  113 us
    ppermute x4, waiting for transfers between devices, gather_by_bits(): theirs = lax.ppermute(grown, axis, [(d, d ^ reach) for d in range(ways)])  67 us
    all_gather x1, blocking collectives, body(): all_dest = lax.all_gather(dest, 'wide', axis=0, tiled=True)  59.4 us
    scatter x1, other arithmetic, body(): jnp.zeros((node_dev + 1, feature_width), jnp.bfloat16).at[local]  55.9 us
    gather x2, local copies, waits for them, and re-layouts, body(): jnp.take_along_axis(grid_values, order[:, :, :, None, None], axis=1)  14.3 us
    gather x4, local copies, waits for them, and re-layouts, aggregate(): picked = jnp.take(piece_tiles, jnp.clip(cols, 0, tile_count - 1), axis=0)  13.7 us
    dot_general x4, matrix products, aggregate(): jnp.einsum('gruij,gujw->riw', values, picked, preferred_element_type=jnp....  12.3 us
    ppermute x4, starting transfers between devices, gather_by_bits(): theirs = lax.ppermute(grown, axis, [(d, d ^ reach) for d in range(ways)])  7.82 us
  transfers between devices with their start and end apart: 6, of which 6 were waited for; matrix products, arithmetic and copies ran while one was open for 6% of the time, Pallas kernels for 0%

profile of v1, /device:TPU:0, one launch (start us, length us, event | category | flops | bytes accessed | tf_op | source)
XLA Modules:
  0.0 371.0 jit_solution(17542973434701372186)
XLA Ops:
  6.5 0.5 collective-permute-start
  7.0 1.4 collective-permute-done
  8.4 1.2 maximum_select_fusion.4
  9.6 3.0 collective-permute-start.1
  12.5 12.2 %collective-permute-done.1 = bf16[2048,128]{1,0:T(8,128)(2,1)S(1)} collective-permute-done((bf16[2048,128]{1,0:T(8,128)(2,1)S(1)}, bf16[2048,128]{1,0:T(8,128)(2,1)S(1)}, u32[]{:S(2)}, u32[]{:S(2)}) %collective-permute-start.1) | collective-permute-done | bytes 524320 | tf_op jit(solution)/shard_map/ppermute | solution.py:12
  24.8 0.3 maximum_select_fusion.3
  25.0 1.9 collective-permute-start.2
  26.9 23.0 %collective-permute-done.2 = bf16[4096,128]{1,0:T(8,128)(2,1)} collective-permute-done((bf16[4096,128]{1,0:T(8,128)(2,1)S(1)}, bf16[4096,128]{1,0:T(8,128)(2,1)}, u32[]{:S(2)}, u32[]{:S(2)}) %collective-permute-start.2) | collective-permute-done | bytes 1048608 | tf_op jit(solution)/shard_map/ppermute | solution.py:12
  49.9 2.1 maximum_select_fusion.2
  52.0 2.6 collective-permute-start.3
  54.5 59.4 %all_gather.9 = s32[16384]{0:T(1024)S(1)} all-gather(s32[1024]{0:T(1024)S(1)} %copy-done.3), channel_id=1, replica_groups=mesh['groups'=2,'wide'=16] {'wide'}, dimensions={0}, use_global_device_ids=true | all-gather | bytes 69632 | tf_op jit(solution)/shard_map/all_gather | solution.py:33
  114.0 30.4 %collective-permute-done.3 = bf16[8192,128]{1,0:T(8,128)(2,1)} collective-permute-done((bf16[8192,128]{1,0:T(8,128)(2,1)S(1)}, bf16[8192,128]{1,0:T(8,128)(2,1)}, u32[]{:S(2)}, u32[]{:S(2)}) %collective-permute-start.3) | collective-permute-done | bytes 2097184 | tf_op jit(solution)/shard_map/ppermute | solution.py:12
  144.3 55.9 %scatter_custom_fusion = bf16[1025,128]{1,0:T(8,128)(2,1)S(1)} fusion(s32[16384]{0:T(1024)S(1)} %compare_select_fusion, bf16[8192,128]{1,0:T(8,128)(2,1)} %collective-permute-done.3, bf16[]{:T(256)} %constant.110, bf16[8192,128]{1,0:T(8,128)(2,1)S(1)} %maximum_select_fusion.2, pred[]{:T(512)S(6)} %eq.12, bf16[]{:T(256)} %constant.81.clone.1), kind=kCustom, calls=%fused_computation.12 | custom fusion | flops 18874368 | bytes 4456709 | tf_op jit(solution)/shard_map/scatter | solution.py:37
  200.2 0.7 slice.22
  201.0 0.2 all-gather.5.cloned.1.call-start
  201.2 0.1 reshape.122
  202.5 5.3 %sort.17 = (s32[16,8,2]{2,1,0:T(8,128)}, s32[16,8,2]{2,1,0:T(8,128)S(1)}) sort(s32[16,8,2]{2,1,0:T(8,128)S(1)} %reshape.122, s32[16,8,2]{2,1,0:T(8,128)S(1)} %iota.16), dimensions={1}, to_apply=%region_0.1 | sort | flops 2048 | bytes 4096 | tf_op jit(solution)/shard_map/jit(argsort)/sort | solution.py:40
  207.8 0.1 reshape.161
  207.9 14.2 %gather_fusion = bf16[256,128,128]{2,1,0:T(8,128)(2,1)} fusion(bf16[16,8,2,128,128]{4,3,2,1,0:T(8,128)(2,1)} %bitcast.79, s32[256]{0:T(256)S(1)} %reshape.161), kind=kCustom, calls=%fused_computation.4 | custom fusion | bytes 16780288 | tf_op jit(solution)/shard_map/jit(take_along_axis)/gather | solution.py:42
  222.1 39.3 %all-gather.3.cloned.1.call-done = bf16[16384,128]{1,0:T(8,128)(2,1)} async-done(((bf16[1024,128]{1,0:T(8,128)(2,1)}), bf16[16384,128]{1,0:T(8,128)(2,1)}) %all-gather.3.cloned.1.call-update) | async-done | bytes 4194320 | tf_op jit(solution)/shard_map/all_gather | solution.py:49
  261.5 2.8 gather_fusion.2
  264.3 2.8 gather_fusion.1
  267.2 3.7 fusion.22
  270.9 0.9 copy-done.1
  271.8 1.4 fusion.25
  273.2 1.1 fusion.20
  274.3 73.5 %all-gather.5.cloned.1.call-done = bf16[16384,256]{1,0:T(8,128)(2,1)} async-done(((bf16[1024,256]{1,0:T(8,128)(2,1)}), bf16[16384,256]{1,0:T(8,128)(2,1)}) %all-gather.5.cloned.1.call-update) | async-done | bytes 8388624 | tf_op jit(solution)/shard_map/all_gather | solution.py:49
  347.9 4.0 %gather_fusion.4 = bf16[16,128,256]{2,1,0:T(8,128)(2,1)S(1)} fusion(bf16[128,128,256]{2,1,0:T(8,128)(2,1)} %bitcast.86, s32[1024]{0:T(1024)S(1)} %pad_clamp_fusion), kind=kCustom, calls=%fused_computation.3.clone | custom fusion | bytes 2097216 | tf_op jit(solution)/shard_map/jit(_take)/gather | solution.py:65
  351.9 4.0 %gather_fusion.3 = bf16[16,128,256]{2,1,0:T(8,128)(2,1)S(1)} fusion(bf16[128,128,256]{2,1,0:T(8,128)(2,1)} %bitcast.87, s32[1024]{0:T(1024)S(1)} %pad_clamp_fusion.1), kind=kCustom, calls=%fused_computation.1.clone | custom fusion | bytes 2097216 | tf_op jit(solution)/shard_map/jit(_take)/gather | solution.py:65
  355.9 3.6 fusion.15
  359.5 3.6 fusion.19
  363.1 1.1 fusion.21
  (42 shorter events, 1.2 us)
Async XLA Ops:
  6.5 356.5 %copy-start = (bf16[256,256]{1,0:T(8,128)(2,1)S(1)}, bf16[256,256]{1,0:T(8,128)(2,1)}, u32[]{:S(2)}) copy-start(bf16[256,256]{1,0:T(8,128)(2,1)} %param.20) | copy-start | bytes 393220
  6.5 48.0 %copy-start.3 = (s32[1024]{0:T(1024)S(1)}, s32[1024]{0:T(1024)}, u32[]{:S(2)}) copy-start(s32[1024]{0:T(1024)} %param.14) | copy-start | bytes 12292
  6.5 254.9 %all-gather.3.cloned.1.call-start = ((), (), s32[]{:S(2)}) async-start(), calls=%async_computation | async-start | bytes 4456448 | tf_op jit(solution)/shard_map/all_gather | solution.py:49
  6.5 1.8 collective-permute-start
  9.6 15.2 %collective-permute-start.1 = (bf16[2048,128]{1,0:T(8,128)(2,1)S(1)}, bf16[2048,128]{1,0:T(8,128)(2,1)S(1)}, u32[]{:S(2)}, u32[]{:S(2)}) collective-permute-start(bf16[2048,128]{1,0:T(8,128)(2,1)S(1)} %maximum_select_fusion.4), channel_id=1, source_target_pairs={{0,2},{1,3},{2,0},{3,1},{4,6},{5,7},{6,4},{7,5},{8,10},{9,11},{10,... | collective-permute-start | bytes 1572872 | tf_op jit(solution)/shard_map/ppermute | solution.py:12
  25.0 24.9 %collective-permute-start.2 = (bf16[4096,128]{1,0:T(8,128)(2,1)S(1)}, bf16[4096,128]{1,0:T(8,128)(2,1)}, u32[]{:S(2)}, u32[]{:S(2)}) collective-permute-start(bf16[4096,128]{1,0:T(8,128)(2,1)S(1)} %maximum_select_fusion.3), channel_id=1, source_target_pairs={{0,4},{1,5},{2,6},{3,7},{4,0},{5,1},{6,2},{7,3},{8,12},{9,13},{10,... | collective-permute-start | bytes 3145736 | tf_op jit(solution)/shard_map/ppermute | solution.py:12
  26.9 174.3 %copy-start.4 = (s32[256]{0:T(256)S(1)}, s32[256]{0:T(256)}, u32[]{:S(2)}) copy-start(s32[256]{0:T(256)} %param.16) | copy-start | bytes 3076
  26.9 174.5 %copy-start.5 = (s32[256]{0:T(256)S(1)}, s32[256]{0:T(256)}, u32[]{:S(2)}) copy-start(s32[256]{0:T(256)} %param.17) | copy-start | bytes 3076
  52.0 92.4 %collective-permute-start.3 = (bf16[8192,128]{1,0:T(8,128)(2,1)S(1)}, bf16[8192,128]{1,0:T(8,128)(2,1)}, u32[]{:S(2)}, u32[]{:S(2)}) collective-permute-start(bf16[8192,128]{1,0:T(8,128)(2,1)S(1)} %maximum_select_fusion.2), channel_id=1, source_target_pairs={{0,8},{1,9},{2,10},{3,11},{4,12},{5,13},{6,14},{7,15},{8,0},{9,1},... | collective-permute-start | bytes 6291464 | tf_op jit(solution)/shard_map/ppermute | solution.py:12
  201.0 146.9 %all-gather.5.cloned.1.call-start = ((), (), s32[]{:S(2)}) async-start(), calls=%async_computation.1 | async-start | bytes 8912896 | tf_op jit(solution)/shard_map/all_gather | solution.py:49
  267.2 4.6 %copy-start.1 = (bf16[256,128,128]{2,1,0:T(8,128)(2,1)S(1)}, bf16[256,128,128]{2,1,0:T(8,128)(2,1)}, u32[]{:S(2)}) copy-start(bf16[256,128,128]{2,1,0:T(8,128)(2,1)} %gather_fusion) | copy-start | bytes 25165828
  271.8 1.4 copy-start.2
  271.8 1.4 copy-start.6
  359.5 3.6 copy-start.7
Sparse Core Ops, SparseCore 0:
  201.1 60.3 all-gather.2
  274.4 73.3 all-gather.4
